TPU v7x, 32 devices: a whole 2x2x4 slice. The times are simulated.
32 devices in a mesh: row: 4 (over x, core), col: 8 (over z, y).
Axes of the slice: x: 2, y: 2, z: 4, core: 2. Of those that a mesh axis runs over, the one named last changes fastest.
Arguments:
- features: bfloat16 [4096, 768], P(('row', 'col')), may hold values from -6 to 6
- self_weight: bfloat16 [768, 768], replicated, may hold values from -0.21875 to 0.21875
- rel_weight: bfloat16 [768, 5, 768], replicated, may hold values from -0.21875 to 0.21875
- bias: float32 [768], replicated, may hold values from -3 to 3
- blocks: bfloat16 [4, 8, 5, 8, 128, 128], P('row', 'col'), may hold values from -0.083496094 to 0.083496094
- block_rows: int32 [4, 8, 5, 8], P('row', 'col'), may hold values from 0 to 7
- block_cols: int32 [4, 8, 5, 8], P('row', 'col'), may hold values from 0 to 3
- block_counts: int32 [4, 8, 5], P('row', 'col'), may hold values from 1 to 8, as said below
Outputs:
- layer_out: bfloat16 [4096, 768], P(('row', 'col'))
Inputs may be any that keep to these rules, and one draw needn't show every extreme that they name: The live slots of a tile and relation are its first block_counts slots; the others are ignored. `block_rows`: pairs of destination and source blocks may repeat within a tile.
All inputs are finite; a program needn't handle non-finite values.
Results may differ from a plain program's by a relative error of at most 0.014.
Values may be sent and summed in bfloat16 or wider, within the bound.
A program may use at most 128 MiB of HBM per device.

v0:
```python
import jax
import jax.numpy as jnp
from jax import lax
from jax.sharding import PartitionSpec as P


def aggregate_tile(tile_blocks, tile_rows, tile_cols, tile_counts, panel, brows):
    relations = tile_blocks.shape[0]
    slots = tile_blocks.shape[1]
    block_size = tile_blocks.shape[-1]
    width = panel.shape[-1]
    total = jnp.zeros((brows, block_size, width), jnp.float32)
    for relation in range(relations):
        source = panel[:, :, relation, :]
        chosen = source[tile_cols[relation]]
        live = lax.iota(jnp.int32, slots) < tile_counts[relation]
        owners = (
            (tile_rows[relation][None, :] == lax.iota(jnp.int32, brows)[:, None]) & live[None, :]
        ).astype(jnp.bfloat16)
        products = jnp.einsum(
            "sik,skd->sid", tile_blocks[relation], chosen, preferred_element_type=jnp.float32
        )
        upper = products.astype(jnp.bfloat16)
        lower = (products - upper.astype(jnp.float32)).astype(jnp.bfloat16)
        halves = jnp.stack([upper, lower], axis=1)
        routed = jnp.einsum("ns,shid->nid", owners, halves, preferred_element_type=jnp.float32)
        total = total + routed
    return total.reshape(brows * block_size, width)


def per_device(
    features, self_weight, rel_weight, bias, blocks, block_rows, block_cols, block_counts
):
    rows_dev, width = features.shape
    relations = rel_weight.shape[1]
    block_size = blocks.shape[-1]
    brows = rows_dev * lax.axis_size("col") // block_size
    bcols = rows_dev * lax.axis_size("row") // block_size
    stacked = rel_weight.reshape(width, relations * width)
    own_rows = jnp.dot(features, stacked, preferred_element_type=jnp.float32).astype(jnp.bfloat16)
    panel = lax.all_gather(own_rows, "row", axis=0, tiled=True)
    panel = panel.reshape(bcols, block_size, relations, width)
    partial_rows = aggregate_tile(
        blocks[0, 0], block_rows[0, 0], block_cols[0, 0], block_counts[0, 0], panel, brows
    )
    owned_sum = lax.psum_scatter(
        partial_rows.astype(jnp.bfloat16), "col", scatter_dimension=0, tiled=True
    ).astype(jnp.float32)
    self_term = jnp.dot(features, self_weight, preferred_element_type=jnp.float32)
    return jnp.maximum(self_term + owned_sum + bias, 0.0).astype(jnp.bfloat16)


def solution(mesh):
    return jax.shard_map(
        per_device,
        mesh=mesh,
        in_specs=(
            P(("row", "col"), None),
            P(),
            P(),
            P(),
            P("row", "col", None, None, None, None),
            P("row", "col", None, None),
            P("row", "col", None, None),
            P("row", "col", None),
        ),
        out_specs=P(("row", "col"), None),
        check_vma=False,
    )
```

profile of v0, /device:TPU:0, one launch (start us, length us, event | category | flops | bytes accessed | tf_op | source)
XLA Modules:
  0.0 219.1 jit_solution(5401067404619747937)
XLA Ops:
  6.5 9.2 %copy.23 = bf16[768,5,768]{0,2,1:T(8,128)(2,1)} copy(bf16[768,5,768]{2,0,1:T(8,128)(2,1)} %param.10) | data formatting | bytes 11796480 | tf_op args[2]
  15.7 5.7 %convolution_convert_fusion = bf16[128,3840]{1,0:T(8,128)(2,1)} fusion(bf16[128,768]{1,0:T(8,128)(2,1)S(1)} %copy-done.11, bf16[768,3840]{0,1:T(8,128)(2,1)} %bitcast.163), kind=kOutput, calls=%fused_computation.10 | convolution fusion | flops 755466240 | bytes 7077888 | tf_op jit(solution)/shard_map/dot_general | solution.py:40
  21.5 0.6 fusion.68
  22.2 1.2 iota_compare_fusion.8
  23.4 1.1 iota_compare_fusion.7
  24.5 1.2 iota_compare_fusion.6
  25.7 1.2 iota_compare_fusion.9
  26.9 1.2 iota_compare_fusion.5
  29.3 28.0 %all-gather.2.cloned.1.call-done = bf16[512,3840]{1,0:T(8,128)(2,1)} async-done(((bf16[128,3840]{1,0:T(8,128)(2,1)}), bf16[512,3840]{1,0:T(8,128)(2,1)}) %all-gather.2.cloned.1.call-update) | async-done | bytes 3932176 | tf_op jit(solution)/shard_map/all_gather | solution.py:41
  57.3 6.3 %copy.24 = bf16[512,3840]{0,1:T(8,128)(2,1)} copy(bf16[512,3840]{1,0:T(8,128)(2,1)} %all-gather.2.cloned.1.call-done) | data formatting | bytes 7864320 | tf_op jit(solution)/shard_map/all_gather | solution.py:41
  63.6 7.6 %reshape.210 = bf16[4,128,5,768]{1,0,3,2:T(4,128)(2,1)} reshape(bf16[512,3840]{0,1:T(8,128)(2,1)} %copy.24) | data formatting | bytes 7864320 | tf_op jit(solution)/shard_map/reshape | solution.py:42
  71.2 3.9 %fusion.67 = (bf16[4,128,1,768]{1,0,3,2:T(4,128)(2,1)}, bf16[4,128,1,768]{1,0,3,2:T(4,128)(2,1)}, bf16[4,128,1,768]{1,0,3,2:T(4,128)(2,1)}, bf16[4,128,1,768]{1,0,3,2:T(4,128)(2,1)S(1)}, bf16[4,128,1,768]{1,0,3,2:T(4,128)(2,1)}) fusion(bf16[4,128,5,768]{1,0,3,2:T(4,128)(2,1)} %reshape.210), kind=kLoop, calls=%fused_computation.110 | loop fusion | bytes 7864320 | tf_op jit(solution)/shard_map/slice | solution.py:14
  75.7 0.8 gather_fusion.1
  76.5 1.6 fusion.24
  78.1 1.4 fusion.14
  79.5 1.4 fusion.6
  81.6 0.6 gather_fusion.2
  82.2 1.6 fusion.22
  83.8 1.4 fusion.15
  85.3 1.4 fusion.7
  87.3 0.6 gather_fusion.3
  88.0 1.6 fusion.20
  89.6 1.4 fusion.16
  91.0 1.5 fusion.8
  93.7 1.6 fusion.18
  95.3 1.5 fusion.17
  96.8 1.4 fusion.9
  99.5 1.6 fusion.26
  101.1 1.4 fusion.13
  102.5 1.5 fusion.5
  105.0 1.9 convert_reduce_fusion.3
  106.8 2.2 copy.30
  109.0 4.1 %convert_reduce_fusion.2 = bf16[8,128,768]{1,2,0:T(8,128)(2,1)} fusion(bf16[8,1,128,768]{2,3,0,1:T(8,128)(2,1)} %fusion.7, bf16[8,1,128,768]{2,3,0,1:T(8,128)(2,1)} %fusion.15), kind=kLoop, calls=%fused_computation.7 | loop fusion | flops 7077888 | bytes 4718592 | tf_op jit(solution)/shard_map/ns,shid->nid/reduce_sum | solution.py:26
  113.2 2.9 %copy.33 = bf16[8,128,768]{2,0,1:T(8,128)(2,1)} copy(bf16[8,128,768]{1,2,0:T(8,128)(2,1)} %convert_reduce_fusion.2) | data formatting | bytes 3145728 | tf_op jit(solution)/shard_map/ns,shid->nid/reduce_sum | solution.py:26
  116.1 4.1 %convert_reduce_fusion.1 = bf16[8,128,768]{1,2,0:T(8,128)(2,1)} fusion(bf16[8,1,128,768]{2,3,0,1:T(8,128)(2,1)} %fusion.8, bf16[8,1,128,768]{2,3,0,1:T(8,128)(2,1)} %fusion.16), kind=kLoop, calls=%fused_computation.6 | loop fusion | flops 7077888 | bytes 4718592 | tf_op jit(solution)/shard_map/ns,shid->nid/reduce_sum | solution.py:26
  120.2 3.0 %copy.36 = bf16[8,128,768]{2,0,1:T(8,128)(2,1)} copy(bf16[8,128,768]{1,2,0:T(8,128)(2,1)} %convert_reduce_fusion.1) | data formatting | bytes 3145728 | tf_op jit(solution)/shard_map/ns,shid->nid/reduce_sum | solution.py:26
  123.2 4.1 %convert_reduce_fusion = bf16[8,128,768]{1,2,0:T(8,128)(2,1)} fusion(bf16[8,1,128,768]{2,3,0,1:T(8,128)(2,1)} %fusion.9, bf16[8,1,128,768]{2,3,0,1:T(8,128)(2,1)} %fusion.17), kind=kLoop, calls=%fused_computation.5 | loop fusion | flops 7077888 | bytes 4718592 | tf_op jit(solution)/shard_map/ns,shid->nid/reduce_sum | solution.py:26
  127.3 3.0 %copy.39 = bf16[8,128,768]{2,0,1:T(8,128)(2,1)} copy(bf16[8,128,768]{1,2,0:T(8,128)(2,1)} %convert_reduce_fusion) | data formatting | bytes 3145728 | tf_op jit(solution)/shard_map/ns,shid->nid/reduce_sum | solution.py:26
  130.3 4.1 %convert_reduce_fusion.4 = bf16[8,128,768]{1,2,0:T(8,128)(2,1)} fusion(bf16[8,1,128,768]{2,3,0,1:T(8,128)(2,1)} %fusion.5, bf16[8,1,128,768]{2,3,0,1:T(8,128)(2,1)} %fusion.13), kind=kLoop, calls=%fused_computation.9 | loop fusion | flops 7077888 | bytes 4718592 | tf_op jit(solution)/shard_map/ns,shid->nid/reduce_sum | solution.py:26
  134.4 3.0 %copy.27 = bf16[8,128,768]{2,0,1:T(8,128)(2,1)} copy(bf16[8,128,768]{1,2,0:T(8,128)(2,1)} %convert_reduce_fusion.4) | data formatting | bytes 3145728 | tf_op jit(solution)/shard_map/ns,shid->nid/reduce_sum | solution.py:26
  138.0 0.8 copy-done.1
  139.4 0.8 copy-done.2
  140.8 0.8 copy-done.3
  142.2 0.8 copy-done.6
  143.0 0.9 add_convert_fusion
  143.9 1.5 copy.40
  145.4 64.9 %reduce-scatter.2.cloned.1.call-done = bf16[128,768]{1,0:T(8,128)(2,1)} async-done(((bf16[1024,768]{1,0:T(8,128)(2,1)}), bf16[128,768]{1,0:T(8,128)(2,1)}) %reduce-scatter.2.cloned.1.call-update) | async-done | bytes 196624 | tf_op jit(solution)/shard_map/reduce_scatter | solution.py:46
  210.3 1.9 fusion.12
  (70 shorter events, 9.0 us)
Async XLA Ops:
  6.5 203.8 %copy-start = (bf16[768,768]{1,0:T(8,128)(2,1)S(1)}, bf16[768,768]{1,0:T(8,128)(2,1)}, u32[]{:S(2)}) copy-start(bf16[768,768]{1,0:T(8,128)(2,1)} %param.9) | copy-start | bytes 3538948
  6.5 9.2 %copy-start.11 = (bf16[128,768]{1,0:T(8,128)(2,1)S(1)}, bf16[128,768]{1,0:T(8,128)(2,1)}, u32[]{:S(2)}) copy-start(bf16[128,768]{1,0:T(8,128)(2,1)} %param.8) | copy-start | bytes 589828
  6.5 50.7 %all-gather.2.cloned.1.call-start = ((), (), s32[]{:S(2)}) async-start(), calls=%async_computation.1 | async-start | bytes 4915200 | tf_op jit(solution)/shard_map/all_gather | solution.py:41
  15.7 5.8 %copy-start.13 = (s32[1,1,5]{2,1,0:T(1,128)S(1)}, s32[1,1,5]{2,1,0:T(1,128)}, u32[]{:S(2)}) copy-start(s32[1,1,5]{2,1,0:T(1,128)} %param.15) | copy-start | bytes 64
  15.7 12.4 %copy-start.15 = (s32[1,1,5,8]{3,1,2,0:T(1,128)S(1)}, s32[1,1,5,8]{3,1,2,0:T(1,128)}, u32[]{:S(2)}) copy-start(s32[1,1,5,8]{3,1,2,0:T(1,128)} %param.14) | copy-start | bytes 484
  15.7 13.0 %copy-start.16 = (s32[1,1,5,8]{3,1,2,0:T(1,128)S(1)}, s32[1,1,5,8]{3,1,2,0:T(1,128)}, u32[]{:S(2)}) copy-start(s32[1,1,5,8]{3,1,2,0:T(1,128)} %param.13) | copy-start | bytes 484
  21.4 188.8 %reduce-scatter.2.cloned.1.call-start = ((), (), s32[]{:S(2)}) async-start(), calls=%async_computation.2 | async-start | bytes 1769472 | tf_op jit(solution)/shard_map/reduce_scatter | solution.py:46
  79.5 1.4 copy-start.10
  85.3 1.4 copy-start.9
  91.0 1.5 copy-start.8
  96.8 1.5 copy-start.7
  102.5 1.9 copy-start.4
  102.5 2.4 %copy-start.5 = (bf16[8,1,128,768]{2,3,0,1:T(8,128)(2,1)S(1)}, bf16[8,1,128,768]{2,3,0,1:T(8,128)(2,1)}, u32[]{:S(2)}) copy-start(bf16[8,1,128,768]{2,3,0,1:T(8,128)(2,1)} %fusion.6) | copy-start | bytes 4718596
  134.4 3.0 %copy-start.21 = (s32[8]{0:T(128)S(1)}, s32[8]{0:T(128)}, u32[]{:S(2)}) copy-start(s32[8]{0:T(128)} %get-tuple-element.12) | copy-start | bytes 100
  134.4 3.0 %copy-start.26 = (pred[8]{0:T(512)(128)(4,1)S(1)}, pred[8]{0:T(512)(128)(4,1)}, u32[]{:S(2)}) copy-start(pred[8]{0:T(512)(128)(4,1)} %iota_compare_fusion.8) | copy-start | bytes 28
  137.4 1.4 copy-start.1
  137.4 1.4 copy-start.20
  137.4 1.4 copy-start.25
  138.8 1.4 copy-start.2
  138.8 1.4 copy-start.19
  138.8 1.4 copy-start.24
  140.2 1.4 copy-start.3
  140.2 1.4 copy-start.18
  140.2 1.4 copy-start.23
  141.6 1.4 copy-start.6
  141.6 1.4 copy-start.17
  141.6 1.4 copy-start.22
  145.3 64.9 %copy-start.12 = (bf16[128,768]{1,0:T(8,128)(2,1)S(1)}, bf16[128,768]{1,0:T(8,128)(2,1)}, u32[]{:S(2)}) copy-start(bf16[128,768]{1,0:T(8,128)(2,1)} %param.8) | copy-start | bytes 589828
  145.4 64.9 %copy-start.14 = (f32[768]{0:T(1024)S(1)}, f32[768]{0:T(1024)}, u32[]{:S(2)}) copy-start(f32[768]{0:T(1024)} %param.11) | copy-start | bytes 9220
Sparse Core Ops, SparseCore 0:
  21.6 35.6 all-gather.1
  145.5 64.7 reduce-scatter.1
where the time goes:
time: 220 us; the launch traced here: 219 us
  waiting for transfers between devices  92.9 us (42%)
  local copies, waits for them, and re-layouts  54.6 us (25%)
  other arithmetic  39.2 us (18%)
  matrix products  18.7 us (8%)
  between operations  13.7 us (6%)
    reduce_scatter x1, waiting for transfers between devices, per_device(): lax.psum_scatter(partial_rows.astype(jnp.bfloat16), 'col', scatter_dimens...  64.9 us
    all_gather x1, waiting for transfers between devices, per_device(): panel = lax.all_gather(own_rows, 'row', axis=0, tiled=True)  28 us
    reduce_sum x5, other arithmetic, aggregate_tile(): jnp.einsum('ns,shid->nid', owners, halves, preferred_element_type=jnp.flo...  18.3 us
    another operation x10, other arithmetic, aggregate_tile(): halves = jnp.stack([upper, lower], axis=1)  14.4 us
    reduce_sum x5, local copies, waits for them, and re-layouts, aggregate_tile(): jnp.einsum('ns,shid->nid', owners, halves, preferred_element_type=jnp.flo...  14.1 us
    unnamed x55, local copies, waits for them, and re-layouts  13.6 us
    dot_general x5, matrix products, aggregate_tile(): jnp.einsum('sik,skd->sid', tile_blocks[relation], chosen, preferred_eleme...  7.95 us
    reshape x1, local copies, waits for them, and re-layouts, per_device(): panel = panel.reshape(bcols, block_size, relations, width)  7.63 us
  transfers between devices with their start and end apart: 2, of which 2 were waited for; matrix products, arithmetic and copies ran while one was open for 4% of the time, Pallas kernels for 0%

commit v1 on v0

v1 whole, which is shorter than its diff:
```python
import functools

import jax
import jax.numpy as jnp
from jax import lax
from jax.experimental import pallas as pl
from jax.experimental.pallas import tpu as pltpu
from jax.sharding import PartitionSpec as P

MESH = pl.DeviceIdType.MESH


def flip(index, mask):
    out = index
    bit = 1
    while bit <= mask:
        if mask & bit:
            out = out + bit - 2 * bit * lax.rem(lax.div(index, bit), 2)
        bit *= 2
    return out


def xor(left, right, size):
    out = 0
    bit = 1
    while bit < size:
        out = out + bit * lax.rem(lax.div(left, bit) + lax.div(right, bit), 2)
        bit *= 2
    return out


def layer_kernel(
    n_row, n_col,
    feat, rows, cols, counts, bias, rel_hbm, self_hbm, blocks_hbm,
    out,
    xbuf, wbuf, swbuf, bbuf, merged, panel, lhs, idx, pairs, own, self_sum, sends, recvs,
    w_sem, sw_sem, b_sem, ag_send, ag_recv, fw_send, fw_recv, rs_send, rs_recv,
):
    block, width = feat.shape
    relations = rel_hbm.shape[0]
    slots = blocks_hbm.shape[0] // relations
    n_pair = n_row // 2
    half = n_col // 2
    n_src = n_row * block
    me_row = lax.axis_index("row")
    me_col = lax.axis_index("col")
    sibling = flip(me_row, 1)
    me_pair = lax.div(me_row, 2)

    b_copy = pltpu.make_async_copy(blocks_hbm, bbuf, b_sem)
    b_copy.start()
    w_copies = []
    for r in range(relations):
        copy = pltpu.make_async_copy(rel_hbm.at[r], wbuf.at[r], w_sem.at[r])
        copy.start()
        w_copies.append(copy)
    sw_copy = pltpu.make_async_copy(self_hbm, swbuf, sw_sem)
    sw_copy.start()

    barrier = pltpu.get_barrier_semaphore()
    row_peers = [sibling] + [flip(me_row, 2 * j) for j in range(1, n_pair)]
    masks = []
    while 2 ** len(masks) < n_col:
        masks.append(2 ** len(masks))
    for peer in row_peers:
        pl.semaphore_signal(barrier, inc=1, device_id={"row": peer}, device_id_type=MESH)
    for mask in masks:
        pl.semaphore_signal(
            barrier, inc=1, device_id={"col": flip(me_col, mask)}, device_id_type=MESH
        )
    pl.semaphore_wait(barrier, len(row_peers) + len(masks))

    def span(row):
        return xbuf.at[pl.ds(pl.multiple_of(row * block, block), block)]

    ag = []
    for j in list(range(1, n_pair)) + [0]:
        copy = pltpu.make_async_remote_copy(
            src_ref=feat, dst_ref=span(me_row), send_sem=ag_send.at[j], recv_sem=ag_recv.at[j],
            device_id={"row": row_peers[j]}, device_id_type=MESH,
        )
        copy.start()
        ag.append(copy)
    ag = [ag[-1]] + ag[:-1]
    xbuf[pl.ds(pl.multiple_of(me_row * block, block), block), :] = feat[...]

    def index_relation(r, carry):
        found = []
        for s in range(slots):
            pair = jnp.where(s < counts[r], rows[r, s] * n_row + cols[r, s], -1)
            found.append(pair)
            pairs[r, s] = pair

        def index_dest(d, inner):
            for k in range(n_row):
                chosen = relations * slots
                for s in range(slots):
                    chosen = jnp.where(found[s] == d * n_row + k, r * slots + s, chosen)
                idx[d, r * n_row + k] = chosen
            return inner

        return lax.fori_loop(0, n_col, index_dest, carry)

    lax.fori_loop(0, relations, index_relation, 0)
    b_copy.wait()
    merged[relations * slots] = jnp.zeros((block, block), merged.dtype)

    def merge_relation(r, carry):
        for s in range(slots):
            total = bbuf[r * slots + s].astype(jnp.float32)
            for t in range(s):
                same = jnp.where(pairs[r, s] == pairs[r, t], 1.0, 0.0).astype(jnp.float32)
                total = total + same * bbuf[r * slots + t].astype(jnp.float32)
            merged[r * slots + s] = total.astype(merged.dtype)
        return carry

    lax.fori_loop(0, relations, merge_relation, 0)

    def transform(pair):
        at = pl.multiple_of(pair * 2 * block, 2 * block)

        def one(r, carry):
            product = jnp.dot(
                xbuf[pl.ds(at, 2 * block), :], wbuf[r], preferred_element_type=jnp.float32
            )
            to = pl.multiple_of(r * n_src + at, 2 * block)
            panel[pl.ds(to, 2 * block), :] = product.astype(panel.dtype)
            return carry

        lax.fori_loop(0, relations, one, 0)

    for copy in w_copies:
        copy.wait()
    ag[0].wait_recv()
    transform(me_pair)
    sw_copy.wait()
    self_sum[...] = (
        jnp.dot(feat[...], swbuf[...], preferred_element_type=jnp.float32) + bias[...]
    )
    forwards = []
    for j in range(1, n_pair):
        ag[j].wait_recv()
        peer = row_peers[j]
        copy = pltpu.make_async_remote_copy(
            src_ref=span(peer), dst_ref=span(peer), send_sem=fw_send.at[j], recv_sem=fw_recv.at[j],
            device_id={"row": sibling}, device_id_type=MESH,
        )
        copy.start()
        forwards.append(copy)
    for j in range(1, n_pair):
        forwards[j - 1].wait_recv()
        transform(lax.div(row_peers[j], 2))

    def partial_sum(e):
        dest = xor(e, me_col, n_col)
        for k in range(relations * n_row):
            lhs[:, k * block:(k + 1) * block] = merged[idx[dest, k]]
        return jnp.dot(lhs[...], panel[...], preferred_element_type=jnp.float32)

    base = [0]
    for _ in masks:
        base.append(base[-1] + (half >> (len(base) - 1)))

    def exchange(stage, slot):
        at = base[stage] + slot
        return pltpu.make_async_remote_copy(
            src_ref=sends.at[at], dst_ref=recvs.at[at],
            send_sem=rs_send.at[at], recv_sem=rs_recv.at[at],
            device_id={"col": flip(me_col, masks[stage])}, device_id_type=MESH,
        )

    def far(t, carry):
        sends[t] = partial_sum(n_col - 1 - 2 * t).astype(sends.dtype)
        exchange(0, t).start()
        return carry

    def near(t, carry):
        own[t] = partial_sum(n_col - 2 - 2 * t)
        return carry

    lax.fori_loop(0, half, far, 0)
    lax.fori_loop(0, half, near, 0)

    for t in range(half):
        exchange(0, t).wait_recv()
        total = own[t] + recvs[t].astype(jnp.float32)
        stage, slot = 1, t
        while stage < len(masks) and slot % 2 == 1:
            slot = slot // 2
            exchange(stage, slot).wait_recv()
            total = total + recvs[base[stage] + slot].astype(jnp.float32)
            stage += 1
        if stage < len(masks):
            sends[base[stage] + slot // 2] = total.astype(sends.dtype)
            exchange(stage, slot // 2).start()
        else:
            out[...] = jnp.maximum(self_sum[...] + total, 0.0).astype(out.dtype)

    for copy in ag + forwards:
        copy.wait_send()
    for stage in range(len(masks)):
        for slot in range(half >> stage):
            exchange(stage, slot).wait_send()


def per_device(
    n_row, n_col,
    features, self_weight, rel_weight, bias, blocks, block_rows, block_cols, block_counts,
):
    block, width = features.shape
    relations = rel_weight.shape[1]
    slots = blocks.shape[3]
    size = blocks.shape[-1]
    bf16, f32, i32 = jnp.bfloat16, jnp.float32, jnp.int32
    vmem = pl.BlockSpec(memory_space=pltpu.VMEM)
    smem = pl.BlockSpec(memory_space=pltpu.SMEM)
    hbm = pl.BlockSpec(memory_space=pl.ANY)
    dma = pltpu.SemaphoreType.DMA
    n_src = n_row * block
    n_pair = n_row // 2
    flops = 2 * width * (n_src * relations * width + block * width)
    flops += 2 * n_col * block * relations * n_src * width
    return pl.pallas_call(
        functools.partial(layer_kernel, n_row, n_col),
        out_shape=jax.ShapeDtypeStruct((block, width), bf16),
        in_specs=[vmem, smem, smem, smem, vmem, hbm, hbm, hbm],
        out_specs=vmem,
        scratch_shapes=[
            pltpu.VMEM((n_src, width), bf16),
            pltpu.VMEM((relations, width, width), bf16),
            pltpu.VMEM((width, width), bf16),
            pltpu.VMEM((relations * slots, size, size), bf16),
            pltpu.VMEM((relations * slots + 1, size, size), bf16),
            pltpu.VMEM((relations * n_src, width), bf16),
            pltpu.VMEM((block, relations * n_src), bf16),
            pltpu.SMEM((n_col, relations * n_row), i32),
            pltpu.SMEM((relations, slots), i32),
            pltpu.VMEM((n_col // 2, block, width), f32),
            pltpu.VMEM((block, width), f32),
            pltpu.VMEM((n_col - 1, block, width), bf16),
            pltpu.VMEM((n_col - 1, block, width), bf16),
            dma((relations,)), dma, dma,
            dma((n_pair,)), dma((n_pair,)), dma((n_pair,)), dma((n_pair,)),
            dma((n_col - 1,)), dma((n_col - 1,)),
        ],
        compiler_params=pltpu.CompilerParams(
            collective_id=0, has_side_effects=True, vmem_limit_bytes=56 * 2 ** 20
        ),
        cost_estimate=pl.CostEstimate(flops=flops, bytes_accessed=9 * 2 ** 20, transcendentals=0),
        name="relational_layer",
    )(
        features, block_rows[0, 0], block_cols[0, 0], block_counts[0, 0], bias.reshape(1, width),
        jnp.transpose(rel_weight, (1, 0, 2)), self_weight,
        blocks.reshape(relations * slots, size, size),
    )


def solution(mesh):
    return jax.shard_map(
        functools.partial(per_device, mesh.shape["row"], mesh.shape["col"]),
        mesh=mesh,
        in_specs=(
            P(("row", "col"), None),
            P(),
            P(),
            P(),
            P("row", "col", None, None, None, None),
            P("row", "col", None, None),
            P("row", "col", None, None),
            P("row", "col", None),
        ),
        out_specs=P(("row", "col"), None),
        check_vma=False,
    )
```

time: 220 us -> 45.6 us (0.21)
  waiting for transfers between devices: 92.9 us -> 0 us
  local copies, waits for them, and re-layouts: 54.6 us -> 4.19 us
  Pallas kernels: 0 us -> 41 us
  other arithmetic: 39.2 us -> 0 us
  matrix products: 18.7 us -> 0 us
  between operations: 13.7 us -> 0.01 us
    reduce_scatter x1 -> x0, waiting for transfers between devices: 64.9 us -> none  [per_device(): lax.psum_scatter(partial_rows.astype(jnp.bfloat16), 'col', scatter_dimens...]
    pallas_call x0 -> x1, Pallas kernels: none -> 41 us  [per_device(): pl.pallas_call(functools.partial(layer_kernel, n_row, n_col), out_shape=j...]
    all_gather x1 -> x0, waiting for transfers between devices: 28 us -> none  [per_device(): panel = lax.all_gather(own_rows, 'row', axis=0, tiled=True)]
    dot_general x12 -> x0, matrix products: 18.7 us -> none  [the longest x5 7.95 us: aggregate_tile(): jnp.einsum('sik,skd->sid', tile_blocks[relation], chosen, preferred_eleme...]
    reduce_sum x5 -> x0, other arithmetic: 18.3 us -> none  [aggregate_tile(): jnp.einsum('ns,shid->nid', owners, halves, preferred_element_type=jnp.flo...]
    another operation x10 -> x0, other arithmetic: 14.4 us -> none  [aggregate_tile(): halves = jnp.stack([upper, lower], axis=1)]
    reduce_sum x5 -> x0, local copies, waits for them, and re-layouts: 14.1 us -> none  [aggregate_tile(): jnp.einsum('ns,shid->nid', owners, halves, preferred_element_type=jnp.flo...]
    unnamed x55 -> x2, local copies, waits for them, and re-layouts: 13.6 us -> 2.91 us
  transfers between devices with their start and end apart: 2 -> 0, of which waited for: 2 -> 0; matrix products, arithmetic and copies ran while one was open for 4% -> 0% of each run, Pallas kernels for 0% -> 0%
where the time goes in v1:
time: 45.6 us; the launch traced here: 45.2 us
  Pallas kernels  41 us (90%)
  local copies, waits for them, and re-layouts  4.19 us (9%)
    pallas_call x1, Pallas kernels, per_device(): pl.pallas_call(functools.partial(layer_kernel, n_row, n_col), out_shape=j...  41 us
    unnamed x2, local copies, waits for them, and re-layouts  2.91 us
    reshape x1, local copies, waits for them, and re-layouts, per_device(): bias.reshape(1, width)  1.28 us

profile of v1, /device:TPU:0, one launch (start us, length us, event | category | flops | bytes accessed | tf_op | source)
XLA Modules:
  0.0 45.2 jit_solution(6152946685177909789)
XLA Ops:
  0.0 1.3 %reshape.6.bias = f32[1,768]{1,0:T(1,128)} reshape(f32[768]{0:T(1024)} %param.11) | data formatting | bytes 6144 | tf_op jit(solution)/shard_map/reshape | solution.py:252
  1.3 1.3 %copy_bitcast_fusion = (s32[5,8]{1,0:T(8,128)}, s32[5,8]{1,0:T(8,128)}) fusion(s32[1,1,5,8]{3,1,2,0:T(1,128)} %param.14, s32[1,1,5,8]{3,1,2,0:T(1,128)} %param.13), kind=kLoop, calls=%fused_computation | loop fusion | bytes 640
  2.6 41.0 %relational_layer.1 = bf16[128,768]{1,0:T(8,128)(2,1)} custom-call(bf16[128,768]{1,0:T(8,128)(2,1)} %feat.1, s32[5,8]{1,0:T(8,128)} %get-tuple-element.6.rows, s32[5,8]{1,0:T(8,128)} %get-tuple-element.5.cols, s32[5]{0:T(128)} %bitcast.9, f32[1,768]{1,0:T(1,128)} %reshape.6.bias, bf16[5,768,768]{2,1,0:T(8,128)(2,1)} %bitcast.7, bf16[768,768]{1,0:T(8,128)(2,1)} %self_hbm.1, ...), custom_call_target="tpu_custom_call" | custom-call | flops 7197425664 | bytes 9437184 | tf_op jit(solution)/shard_map/relational_layer/pallas_call | solution.py:223
  43.6 1.6 %copy.14 = bf16[128,768]{1,0:T(8,128)(2,1)} copy(bf16[128,768]{1,0:T(8,128)(2,1)} %relational_layer.1) | data formatting | bytes 393216

commit v2 on v1

--- a/solution.py
+++ b/solution.py
@@ -42,6 +42,7 @@
     n_pair = n_row // 2
     half = n_col // 2
     n_src = n_row * block
+    parts, _, part = panel.shape
     me_row = lax.axis_index("row")
     me_col = lax.axis_index("col")
     sibling = flip(me_row, 1)
@@ -87,7 +88,7 @@
     def index_relation(r, carry):
         found = []
         for s in range(slots):
-            pair = jnp.where(s < counts[r], rows[r, s] * n_row + cols[r, s], -1)
+            pair = jnp.where(s < counts[0, r], rows[r, 0, s] * n_row + cols[r, 0, s], -1)
             found.append(pair)
             pairs[r, s] = pair
 
@@ -102,29 +103,19 @@
         return lax.fori_loop(0, n_col, index_dest, carry)
 
     lax.fori_loop(0, relations, index_relation, 0)
-    b_copy.wait()
-    merged[relations * slots] = jnp.zeros((block, block), merged.dtype)
-
-    def merge_relation(r, carry):
-        for s in range(slots):
-            total = bbuf[r * slots + s].astype(jnp.float32)
-            for t in range(s):
-                same = jnp.where(pairs[r, s] == pairs[r, t], 1.0, 0.0).astype(jnp.float32)
-                total = total + same * bbuf[r * slots + t].astype(jnp.float32)
-            merged[r * slots + s] = total.astype(merged.dtype)
-        return carry
-
-    lax.fori_loop(0, relations, merge_relation, 0)
-
-    def transform(pair):
+
+    def transform(pair, first, many):
         at = pl.multiple_of(pair * 2 * block, 2 * block)
 
         def one(r, carry):
             product = jnp.dot(
-                xbuf[pl.ds(at, 2 * block), :], wbuf[r], preferred_element_type=jnp.float32
-            )
+                xbuf[pl.ds(at, 2 * block), :],
+                wbuf[r, :, first * part:(first + many) * part],
+                preferred_element_type=jnp.float32,
+            ).astype(panel.dtype)
             to = pl.multiple_of(r * n_src + at, 2 * block)
-            panel[pl.ds(to, 2 * block), :] = product.astype(panel.dtype)
+            for p in range(many):
+                panel[first + p, pl.ds(to, 2 * block), :] = product[:, p * part:(p + 1) * part]
             return carry
 
         lax.fori_loop(0, relations, one, 0)
@@ -132,11 +123,7 @@
     for copy in w_copies:
         copy.wait()
     ag[0].wait_recv()
-    transform(me_pair)
-    sw_copy.wait()
-    self_sum[...] = (
-        jnp.dot(feat[...], swbuf[...], preferred_element_type=jnp.float32) + bias[...]
-    )
+    transform(me_pair, 0, parts)
     forwards = []
     for j in range(1, n_pair):
         ag[j].wait_recv()
@@ -147,60 +134,113 @@
         )
         copy.start()
         forwards.append(copy)
-    for j in range(1, n_pair):
-        forwards[j - 1].wait_recv()
-        transform(lax.div(row_peers[j], 2))
-
-    def partial_sum(e):
-        dest = xor(e, me_col, n_col)
-        for k in range(relations * n_row):
-            lhs[:, k * block:(k + 1) * block] = merged[idx[dest, k]]
-        return jnp.dot(lhs[...], panel[...], preferred_element_type=jnp.float32)
+
+    sw_copy.wait()
+    self_sum[...] = (
+        jnp.dot(feat[...], swbuf[...], preferred_element_type=jnp.float32)
+        + bias[...].reshape(1, width)
+    )
+    b_copy.wait()
+    merged[relations * slots] = jnp.zeros((block, block), merged.dtype)
+
+    def merge_relation(r, carry):
+        for s in range(slots):
+            total = bbuf[r * slots + s].astype(jnp.float32)
+            for t in range(s):
+                same = jnp.where(pairs[r, s] == pairs[r, t], 1.0, 0.0).astype(jnp.float32)
+                total = total + same * bbuf[r * slots + t].astype(jnp.float32)
+            merged[r * slots + s] = total.astype(merged.dtype)
+        return carry
+
+    lax.fori_loop(0, relations, merge_relation, 0)
+
+    orders = [list(masks) for _ in range(parts)]
+    orders[1][:2] = [masks[1], masks[0]]
+
+    def pair_of_sums(p, v, buf):
+        for h in range(2):
+            e = sum(
+                mask * lax.rem(lax.div(v - 2 * h, 2 ** stage), 2)
+                for stage, mask in enumerate(orders[p])
+            )
+            dest = xor(e, me_col, n_col)
+            for k in range(relations * n_row):
+                lhs[buf, h * block:(h + 1) * block, k * block:(k + 1) * block] = merged[idx[dest, k]]
+        return jnp.dot(lhs[buf], panel[p], preferred_element_type=jnp.float32)
 
     base = [0]
     for _ in masks:
         base.append(base[-1] + (half >> (len(base) - 1)))
 
-    def exchange(stage, slot):
+    def exchange(p, stage, slot):
         at = base[stage] + slot
         return pltpu.make_async_remote_copy(
-            src_ref=sends.at[at], dst_ref=recvs.at[at],
-            send_sem=rs_send.at[at], recv_sem=rs_recv.at[at],
-            device_id={"col": flip(me_col, masks[stage])}, device_id_type=MESH,
+            src_ref=sends.at[p, at], dst_ref=recvs.at[p, at],
+            send_sem=rs_send.at[p, at], recv_sem=rs_recv.at[p, at],
+            device_id={"col": flip(me_col, orders[p][stage])}, device_id_type=MESH,
         )
 
-    def far(t, carry):
-        sends[t] = partial_sum(n_col - 1 - 2 * t).astype(sends.dtype)
-        exchange(0, t).start()
-        return carry
-
-    def near(t, carry):
-        own[t] = partial_sum(n_col - 2 - 2 * t)
-        return carry
-
-    lax.fori_loop(0, half, far, 0)
-    lax.fori_loop(0, half, near, 0)
-
-    for t in range(half):
-        exchange(0, t).wait_recv()
-        total = own[t] + recvs[t].astype(jnp.float32)
-        stage, slot = 1, t
+    def receive(p, stage, slot):
+        exchange(p, stage, slot).wait_recv()
+        return recvs[p, base[stage] + slot].astype(jnp.float32)
+
+    def send(p, stage, slot, total):
+        sends[p, base[stage] + slot] = total.astype(sends.dtype)
+        exchange(p, stage, slot).start()
+
+    for j in range(1, n_pair):
+        forwards[j - 1].wait_recv()
+    for p in range(parts):
+        for j in range(1, n_pair):
+            transform(lax.div(row_peers[j], 2), p, 1)
+
+        def far(i, carry):
+            sums = pair_of_sums(p, n_col - 1 - 4 * i, 0)
+            for h in range(2):
+                send(p, 0, 2 * i + h, sums[h * block:(h + 1) * block])
+            return carry
+
+        lax.fori_loop(0, half // 2, far, 0)
+
+    def near(p, i):
+        sums = pair_of_sums(p, n_col - 2 - 4 * i, (p + i) % 2)
+        send(p, 1, i, sums[:block] + receive(p, 0, 2 * i))
+        own[p, i] = sums[block:] + receive(p, 0, 2 * i + 1)
+
+    def deeper(p, i):
+        total = own[p, i] + receive(p, 1, i)
+        stage, slot = 2, i
         while stage < len(masks) and slot % 2 == 1:
             slot = slot // 2
-            exchange(stage, slot).wait_recv()
-            total = total + recvs[base[stage] + slot].astype(jnp.float32)
+            total = total + receive(p, stage, slot)
             stage += 1
         if stage < len(masks):
-            sends[base[stage] + slot // 2] = total.astype(sends.dtype)
-            exchange(stage, slot // 2).start()
+            send(p, stage, slot // 2, total)
         else:
-            out[...] = jnp.maximum(self_sum[...] + total, 0.0).astype(out.dtype)
+            at = slice(p * part, (p + 1) * part)
+            out[:, at] = jnp.maximum(self_sum[:, at] + total, 0.0).astype(out.dtype)
+
+    last = half // 2 - 1
+    for i in range(last + 1):
+        near(0, i)
+        near(1, i)
+        if i < last:
+            deeper(0, i)
+            deeper(1, i)
+    for p in range(2, parts):
+        for i in range(last + 1):
+            near(p, i)
+            if p == 2 and i == 0:
+                deeper(0, last)
+                deeper(1, last)
+            deeper(p, i)
 
     for copy in ag + forwards:
         copy.wait_send()
-    for stage in range(len(masks)):
-        for slot in range(half >> stage):
-            exchange(stage, slot).wait_send()
+    for p in range(parts):
+        for stage in range(len(masks)):
+            for slot in range(half >> stage):
+                exchange(p, stage, slot).wait_send()
 
 
 def per_device(
@@ -218,6 +258,8 @@
     dma = pltpu.SemaphoreType.DMA
     n_src = n_row * block
     n_pair = n_row // 2
+    part = 256
+    parts = width // part
     flops = 2 * width * (n_src * relations * width + block * width)
     flops += 2 * n_col * block * relations * n_src * width
     return pl.pallas_call(
@@ -231,17 +273,17 @@
             pltpu.VMEM((width, width), bf16),
             pltpu.VMEM((relations * slots, size, size), bf16),
             pltpu.VMEM((relations * slots + 1, size, size), bf16),
-            pltpu.VMEM((relations * n_src, width), bf16),
-            pltpu.VMEM((block, relations * n_src), bf16),
+            pltpu.VMEM((parts, relations * n_src, part), bf16),
+            pltpu.VMEM((2, 2 * block, relations * n_src), bf16),
             pltpu.SMEM((n_col, relations * n_row), i32),
             pltpu.SMEM((relations, slots), i32),
-            pltpu.VMEM((n_col // 2, block, width), f32),
+            pltpu.VMEM((parts, n_col // 4, block, part), f32),
             pltpu.VMEM((block, width), f32),
-            pltpu.VMEM((n_col - 1, block, width), bf16),
-            pltpu.VMEM((n_col - 1, block, width), bf16),
+            pltpu.VMEM((parts, n_col - 1, block, part), bf16),
+            pltpu.VMEM((parts, n_col - 1, block, part), bf16),
             dma((relations,)), dma, dma,
             dma((n_pair,)), dma((n_pair,)), dma((n_pair,)), dma((n_pair,)),
-            dma((n_col - 1,)), dma((n_col - 1,)),
+            dma((parts, n_col - 1)), dma((parts, n_col - 1)),
         ],
         compiler_params=pltpu.CompilerParams(
             collective_id=0, has_side_effects=True, vmem_limit_bytes=56 * 2 ** 20
@@ -249,7 +291,8 @@
         cost_estimate=pl.CostEstimate(flops=flops, bytes_accessed=9 * 2 ** 20, transcendentals=0),
         name="relational_layer",
     )(
-        features, block_rows[0, 0], block_cols[0, 0], block_counts[0, 0], bias.reshape(1, width),
+        features, block_rows.reshape(relations, 1, slots), block_cols.reshape(relations, 1, slots),
+        block_counts.reshape(1, relations), bias,
         jnp.transpose(rel_weight, (1, 0, 2)), self_weight,
         blocks.reshape(relations * slots, size, size),
     )

time: 45.6 us -> 43.1 us (0.945)
  local copies, waits for them, and re-layouts: 4.19 us -> 1.62 us
    unnamed x2 -> x1, local copies, waits for them, and re-layouts: 2.91 us -> 1.62 us
    reshape x1 -> x0, local copies, waits for them, and re-layouts: 1.28 us -> none  [per_device(): bias.reshape(1, width)]
where the time goes in v2:
time: 43.1 us; the launch traced here: 43 us
  Pallas kernels  41.4 us (96%)
  local copies, waits for them, and re-layouts  1.62 us (4%)
    pallas_call x1, Pallas kernels, per_device(): pl.pallas_call(functools.partial(layer_kernel, n_row, n_col), out_shape=j...  41.4 us
    unnamed x1, local copies, waits for them, and re-layouts  1.62 us

profile of v2, /device:TPU:0, one launch (start us, length us, event | category | flops | bytes accessed | tf_op | source)
XLA Modules:
  0.0 43.0 jit_solution(8970854464458941222)
XLA Ops:
  0.0 41.4 %relational_layer.1 = bf16[128,768]{1,0:T(8,128)(2,1)} custom-call(bf16[128,768]{1,0:T(8,128)(2,1)} %feat.1, s32[5,1,8]{2,1,0:T(1,128)} %bitcast.7, s32[5,1,8]{2,1,0:T(1,128)} %bitcast.8, s32[1,5]{1,0:T(1,128)} %bitcast.9, f32[768]{0:T(1024)} %bias.1, bf16[5,768,768]{2,1,0:T(8,128)(2,1)} %bitcast.5, bf16[768,768]{1,0:T(8,128)(2,1)} %self_hbm.1, ...), custom_call_target="tpu_custom_call" | custom-call | flops 7197425664 | bytes 9437184 | tf_op jit(solution)/shard_map/relational_layer/pallas_call | solution.py:265
  41.4 1.6 %copy.10 = bf16[128,768]{1,0:T(8,128)(2,1)} copy(bf16[128,768]{1,0:T(8,128)(2,1)} %relational_layer.1) | data formatting | bytes 393216

commit v3 on v2

--- a/solution.py
+++ b/solution.py
@@ -33,8 +33,8 @@
     n_row, n_col,
     feat, rows, cols, counts, bias, rel_hbm, self_hbm, blocks_hbm,
     out,
-    xbuf, wbuf, swbuf, bbuf, merged, panel, lhs, idx, pairs, own, self_sum, sends, recvs,
-    w_sem, sw_sem, b_sem, ag_send, ag_recv, fw_send, fw_recv, rs_send, rs_recv,
+    xbuf, wbuf, swbuf, bbuf, merged, panel, lhs, table, idx, pairs, own, self_sum, sends, recvs,
+    w_sem, sw_sem, b_sem, idx_sem, ag_send, ag_recv, fw_send, fw_recv, rs_send, rs_recv,
 ):
     block, width = feat.shape
     relations = rel_hbm.shape[0]
@@ -48,16 +48,6 @@
     sibling = flip(me_row, 1)
     me_pair = lax.div(me_row, 2)
 
-    b_copy = pltpu.make_async_copy(blocks_hbm, bbuf, b_sem)
-    b_copy.start()
-    w_copies = []
-    for r in range(relations):
-        copy = pltpu.make_async_copy(rel_hbm.at[r], wbuf.at[r], w_sem.at[r])
-        copy.start()
-        w_copies.append(copy)
-    sw_copy = pltpu.make_async_copy(self_hbm, swbuf, sw_sem)
-    sw_copy.start()
-
     barrier = pltpu.get_barrier_semaphore()
     row_peers = [sibling] + [flip(me_row, 2 * j) for j in range(1, n_pair)]
     masks = []
@@ -69,6 +59,16 @@
         pl.semaphore_signal(
             barrier, inc=1, device_id={"col": flip(me_col, mask)}, device_id_type=MESH
         )
+    b_copy = pltpu.make_async_copy(blocks_hbm, bbuf, b_sem)
+    b_copy.start()
+    w_copies = []
+    for r in range(relations):
+        copy = pltpu.make_async_copy(rel_hbm.at[r], wbuf.at[r], w_sem.at[r])
+        copy.start()
+        w_copies.append(copy)
+    sw_copy = pltpu.make_async_copy(self_hbm, swbuf, sw_sem)
+    sw_copy.start()
+
     pl.semaphore_wait(barrier, len(row_peers) + len(masks))
 
     def span(row):
@@ -85,24 +85,20 @@
     ag = [ag[-1]] + ag[:-1]
     xbuf[pl.ds(pl.multiple_of(me_row * block, block), block), :] = feat[...]
 
-    def index_relation(r, carry):
-        found = []
+    lane = lax.broadcasted_iota(jnp.int32, table.shape, 1)
+    dest_row = lax.broadcasted_iota(jnp.int32, table.shape, 0)
+    lane_relation = lax.div(lane, n_row)
+    wanted = (lane_relation * n_col + dest_row) * n_row + lax.rem(lane, n_row)
+    chosen = jnp.full(table.shape, relations * slots, jnp.int32)
+    for r in range(relations):
         for s in range(slots):
-            pair = jnp.where(s < counts[0, r], rows[r, 0, s] * n_row + cols[r, 0, s], -1)
-            found.append(pair)
+            pair = (r * n_col + rows[r, 0, s]) * n_row + cols[r, 0, s]
+            pair = jnp.where(s < counts[0, r], pair, -1)
             pairs[r, s] = pair
-
-        def index_dest(d, inner):
-            for k in range(n_row):
-                chosen = relations * slots
-                for s in range(slots):
-                    chosen = jnp.where(found[s] == d * n_row + k, r * slots + s, chosen)
-                idx[d, r * n_row + k] = chosen
-            return inner
-
-        return lax.fori_loop(0, n_col, index_dest, carry)
-
-    lax.fori_loop(0, relations, index_relation, 0)
+            chosen = jnp.where(wanted == pair, r * slots + s, chosen)
+    table[...] = chosen
+    idx_copy = pltpu.make_async_copy(table, idx, idx_sem)
+    idx_copy.start()
 
     def transform(pair, first, many):
         at = pl.multiple_of(pair * 2 * block, 2 * block)
@@ -141,6 +137,7 @@
         + bias[...].reshape(1, width)
     )
     b_copy.wait()
+    idx_copy.wait()
     merged[relations * slots] = jnp.zeros((block, block), merged.dtype)
 
     def merge_relation(r, carry):
@@ -220,20 +217,18 @@
             at = slice(p * part, (p + 1) * part)
             out[:, at] = jnp.maximum(self_sum[:, at] + total, 0.0).astype(out.dtype)
 
-    last = half // 2 - 1
-    for i in range(last + 1):
+    for i in range(half // 2):
         near(0, i)
         near(1, i)
-        if i < last:
-            deeper(0, i)
-            deeper(1, i)
     for p in range(2, parts):
-        for i in range(last + 1):
+        for i in range(half // 2):
             near(p, i)
             if p == 2 and i == 0:
-                deeper(0, last)
-                deeper(1, last)
-            deeper(p, i)
+                deeper(0, 0)
+    for i in range(half // 2):
+        for p in range(parts):
+            if (p, i) != (0, 0):
+                deeper(p, i)
 
     for copy in ag + forwards:
         copy.wait_send()
@@ -259,6 +254,7 @@
     n_src = n_row * block
     n_pair = n_row // 2
     part = 256
+    lanes = pl.cdiv(relations * n_row, 128) * 128
     parts = width // part
     flops = 2 * width * (n_src * relations * width + block * width)
     flops += 2 * n_col * block * relations * n_src * width
@@ -275,13 +271,14 @@
             pltpu.VMEM((relations * slots + 1, size, size), bf16),
             pltpu.VMEM((parts, relations * n_src, part), bf16),
             pltpu.VMEM((2, 2 * block, relations * n_src), bf16),
-            pltpu.SMEM((n_col, relations * n_row), i32),
+            pltpu.VMEM((n_col, lanes), i32),
+            pltpu.SMEM((n_col, lanes), i32),
             pltpu.SMEM((relations, slots), i32),
             pltpu.VMEM((parts, n_col // 4, block, part), f32),
             pltpu.VMEM((block, width), f32),
             pltpu.VMEM((parts, n_col - 1, block, part), bf16),
             pltpu.VMEM((parts, n_col - 1, block, part), bf16),
-            dma((relations,)), dma, dma,
+            dma((relations,)), dma, dma, dma,
             dma((n_pair,)), dma((n_pair,)), dma((n_pair,)), dma((n_pair,)),
             dma((parts, n_col - 1)), dma((parts, n_col - 1)),
         ],

time: 43.1 us -> 40.5 us (0.940)
  Pallas kernels: 41.4 us -> 38.7 us
    pallas_call x1, Pallas kernels: 41.4 us -> 38.7 us  [per_device(): pl.pallas_call(functools.partial(layer_kernel, n_row, n_col), out_shape=j...]
where the time goes in v3:
time: 40.5 us; the launch traced here: 40.3 us
  Pallas kernels  38.7 us (96%)
  local copies, waits for them, and re-layouts  1.62 us (4%)
    pallas_call x1, Pallas kernels, per_device(): pl.pallas_call(functools.partial(layer_kernel, n_row, n_col), out_shape=j...  38.7 us
    unnamed x1, local copies, waits for them, and re-layouts  1.62 us

profile of v3, /device:TPU:0, one launch (start us, length us, event | category | flops | bytes accessed | tf_op | source)
XLA Modules:
  0.0 40.3 jit_solution(11323190025288576617)
XLA Ops:
  0.0 38.7 %relational_layer.1 = bf16[128,768]{1,0:T(8,128)(2,1)} custom-call(bf16[128,768]{1,0:T(8,128)(2,1)} %feat.1, s32[5,1,8]{2,1,0:T(1,128)} %bitcast.7, s32[5,1,8]{2,1,0:T(1,128)} %bitcast.8, s32[1,5]{1,0:T(1,128)} %bitcast.9, f32[768]{0:T(1024)} %bias.1, bf16[5,768,768]{2,1,0:T(8,128)(2,1)} %bitcast.5, bf16[768,768]{1,0:T(8,128)(2,1)} %self_hbm.1, ...), custom_call_target="tpu_custom_call" | custom-call | flops 7197425664 | bytes 9437184 | tf_op jit(solution)/shard_map/relational_layer/pallas_call | solution.py:261
  38.7 1.6 %copy.10 = bf16[128,768]{1,0:T(8,128)(2,1)} copy(bf16[128,768]{1,0:T(8,128)(2,1)} %relational_layer.1) | data formatting | bytes 393216

commit v4 on v3

--- a/solution.py
+++ b/solution.py
@@ -71,18 +71,23 @@
 
     pl.semaphore_wait(barrier, len(row_peers) + len(masks))
 
-    def span(row):
-        return xbuf.at[pl.ds(pl.multiple_of(row * block, block), block)]
-
-    ag = []
-    for j in list(range(1, n_pair)) + [0]:
+    part_rows = block // 2
+
+    def span(row, h, many):
+        at = pl.multiple_of(row * block + h * part_rows, part_rows)
+        return xbuf.at[pl.ds(at, many * part_rows)]
+
+    def gather(j, h, many):
         copy = pltpu.make_async_remote_copy(
-            src_ref=feat, dst_ref=span(me_row), send_sem=ag_send.at[j], recv_sem=ag_recv.at[j],
+            src_ref=feat.at[pl.ds(h * part_rows, many * part_rows)], dst_ref=span(me_row, h, many),
+            send_sem=ag_send.at[j, h], recv_sem=ag_recv.at[j, h],
             device_id={"row": row_peers[j]}, device_id_type=MESH,
         )
         copy.start()
-        ag.append(copy)
-    ag = [ag[-1]] + ag[:-1]
+        return copy
+
+    ag = [(j, h, gather(j, h, 1)) for j in range(1, n_pair) for h in range(2)]
+    near_copy = gather(0, 0, 2)
     xbuf[pl.ds(pl.multiple_of(me_row * block, block), block), :] = feat[...]
 
     lane = lax.broadcasted_iota(jnp.int32, table.shape, 1)
@@ -118,24 +123,8 @@
 
     for copy in w_copies:
         copy.wait()
-    ag[0].wait_recv()
+    near_copy.wait_recv()
     transform(me_pair, 0, parts)
-    forwards = []
-    for j in range(1, n_pair):
-        ag[j].wait_recv()
-        peer = row_peers[j]
-        copy = pltpu.make_async_remote_copy(
-            src_ref=span(peer), dst_ref=span(peer), send_sem=fw_send.at[j], recv_sem=fw_recv.at[j],
-            device_id={"row": sibling}, device_id_type=MESH,
-        )
-        copy.start()
-        forwards.append(copy)
-
-    sw_copy.wait()
-    self_sum[...] = (
-        jnp.dot(feat[...], swbuf[...], preferred_element_type=jnp.float32)
-        + bias[...].reshape(1, width)
-    )
     b_copy.wait()
     idx_copy.wait()
     merged[relations * slots] = jnp.zeros((block, block), merged.dtype)
@@ -151,6 +140,22 @@
 
     lax.fori_loop(0, relations, merge_relation, 0)
 
+    forwards = []
+    for j, h, copy in ag:
+        copy.wait_recv()
+        at = span(row_peers[j], h, 1)
+        copy = pltpu.make_async_remote_copy(
+            src_ref=at, dst_ref=at, send_sem=fw_send.at[j, h], recv_sem=fw_recv.at[j, h],
+            device_id={"row": sibling}, device_id_type=MESH,
+        )
+        copy.start()
+        forwards.append(copy)
+
+    sw_copy.wait()
+    self_sum[...] = (
+        jnp.dot(feat[...], swbuf[...], preferred_element_type=jnp.float32)
+        + bias[...].reshape(1, width)
+    )
     orders = [list(masks) for _ in range(parts)]
     orders[1][:2] = [masks[1], masks[0]]
 
@@ -185,8 +190,8 @@
         sends[p, base[stage] + slot] = total.astype(sends.dtype)
         exchange(p, stage, slot).start()
 
-    for j in range(1, n_pair):
-        forwards[j - 1].wait_recv()
+    for copy in forwards:
+        copy.wait_recv()
     for p in range(parts):
         for j in range(1, n_pair):
             transform(lax.div(row_peers[j], 2), p, 1)
@@ -230,7 +235,7 @@
             if (p, i) != (0, 0):
                 deeper(p, i)
 
-    for copy in ag + forwards:
+    for copy in [near_copy] + [copy for _, _, copy in ag] + forwards:
         copy.wait_send()
     for p in range(parts):
         for stage in range(len(masks)):
@@ -279,7 +284,7 @@
             pltpu.VMEM((parts, n_col - 1, block, part), bf16),
             pltpu.VMEM((parts, n_col - 1, block, part), bf16),
             dma((relations,)), dma, dma, dma,
-            dma((n_pair,)), dma((n_pair,)), dma((n_pair,)), dma((n_pair,)),
+            dma((n_pair, 2)), dma((n_pair, 2)), dma((n_pair, 2)), dma((n_pair, 2)),
             dma((parts, n_col - 1)), dma((parts, n_col - 1)),
         ],
         compiler_params=pltpu.CompilerParams(

time: 40.5 us -> 40.6 us (level)
  no operation moved by 1% of the time
where the time goes in v4:
time: 40.6 us; the launch traced here: 40.4 us
  Pallas kernels  38.8 us (96%)
  local copies, waits for them, and re-layouts  1.62 us (4%)
    pallas_call x1, Pallas kernels, per_device(): pl.pallas_call(functools.partial(layer_kernel, n_row, n_col), out_shape=j...  38.8 us
    unnamed x1, local copies, waits for them, and re-layouts  1.62 us

profile of v4, /device:TPU:0, one launch (start us, length us, event | category | flops | bytes accessed | tf_op | source)
XLA Modules:
  0.0 40.4 jit_solution(279459432529873616)
XLA Ops:
  0.0 38.8 %relational_layer.1 = bf16[128,768]{1,0:T(8,128)(2,1)} custom-call(bf16[128,768]{1,0:T(8,128)(2,1)} %feat.1, s32[5,1,8]{2,1,0:T(1,128)} %bitcast.7, s32[5,1,8]{2,1,0:T(1,128)} %bitcast.8, s32[1,5]{1,0:T(1,128)} %bitcast.9, f32[768]{0:T(1024)} %bias.1, bf16[5,768,768]{2,1,0:T(8,128)(2,1)} %bitcast.5, bf16[768,768]{1,0:T(8,128)(2,1)} %self_hbm.1, ...), custom_call_target="tpu_custom_call" | custom-call | flops 7197425664 | bytes 9437184 | tf_op jit(solution)/shard_map/relational_layer/pallas_call | solution.py:266
  38.8 1.6 %copy.10 = bf16[128,768]{1,0:T(8,128)(2,1)} copy(bf16[128,768]{1,0:T(8,128)(2,1)} %relational_layer.1) | data formatting | bytes 393216

commit v5 on v3

--- a/solution.py
+++ b/solution.py
@@ -154,8 +154,15 @@
     orders = [list(masks) for _ in range(parts)]
     orders[1][:2] = [masks[1], masks[0]]
 
+    cached = lhs.shape[0] > 2
+
     def pair_of_sums(p, v, buf):
-        for h in range(2):
+        own_rows = not cached or p < 2
+        if cached and p == 1:
+            buf = half + lax.rem(buf, 2)
+        elif not cached:
+            buf = lax.rem(buf, 2)
+        for h in range(2 if own_rows else 0):
             e = sum(
                 mask * lax.rem(lax.div(v - 2 * h, 2 ** stage), 2)
                 for stage, mask in enumerate(orders[p])
@@ -192,7 +199,7 @@
             transform(lax.div(row_peers[j], 2), p, 1)
 
         def far(i, carry):
-            sums = pair_of_sums(p, n_col - 1 - 4 * i, 0)
+            sums = pair_of_sums(p, n_col - 1 - 4 * i, i)
             for h in range(2):
                 send(p, 0, 2 * i + h, sums[h * block:(h + 1) * block])
             return carry
@@ -200,7 +207,7 @@
         lax.fori_loop(0, half // 2, far, 0)
 
     def near(p, i):
-        sums = pair_of_sums(p, n_col - 2 - 4 * i, (p + i) % 2)
+        sums = pair_of_sums(p, n_col - 2 - 4 * i, half // 2 + i)
         send(p, 1, i, sums[:block] + receive(p, 0, 2 * i))
         own[p, i] = sums[block:] + receive(p, 0, 2 * i + 1)
 
@@ -254,6 +261,8 @@
     n_src = n_row * block
     n_pair = n_row // 2
     part = 256
+    rows_bytes = 4 * block * relations * n_src
+    buffers = n_col // 2 + 2 if (n_col // 2 + 2) * rows_bytes < 16 * 2 ** 20 else 2
     lanes = pl.cdiv(relations * n_row, 128) * 128
     parts = width // part
     flops = 2 * width * (n_src * relations * width + block * width)
@@ -270,7 +279,7 @@
             pltpu.VMEM((relations * slots, size, size), bf16),
             pltpu.VMEM((relations * slots + 1, size, size), bf16),
             pltpu.VMEM((parts, relations * n_src, part), bf16),
-            pltpu.VMEM((2, 2 * block, relations * n_src), bf16),
+            pltpu.VMEM((buffers, 2 * block, relations * n_src), bf16),
             pltpu.VMEM((n_col, lanes), i32),
             pltpu.SMEM((n_col, lanes), i32),
             pltpu.SMEM((relations, slots), i32),

time: 40.5 us -> 40.5 us (level)
  no operation moved by 1% of the time
where the time goes in v5:
time: 40.5 us; the launch traced here: 40.4 us
  Pallas kernels  38.7 us (96%)
  local copies, waits for them, and re-layouts  1.62 us (4%)
    pallas_call x1, Pallas kernels, per_device(): pl.pallas_call(functools.partial(layer_kernel, n_row, n_col), out_shape=j...  38.7 us
    unnamed x1, local copies, waits for them, and re-layouts  1.62 us

profile of v5, /device:TPU:0, one launch (start us, length us, event | category | flops | bytes accessed | tf_op | source)
XLA Modules:
  0.0 40.4 jit_solution(12365622749787976540)
XLA Ops:
  0.0 38.7 %relational_layer.1 = bf16[128,768]{1,0:T(8,128)(2,1)} custom-call(bf16[128,768]{1,0:T(8,128)(2,1)} %feat.1, s32[5,1,8]{2,1,0:T(1,128)} %bitcast.7, s32[5,1,8]{2,1,0:T(1,128)} %bitcast.8, s32[1,5]{1,0:T(1,128)} %bitcast.9, f32[768]{0:T(1024)} %bias.1, bf16[5,768,768]{2,1,0:T(8,128)(2,1)} %bitcast.5, bf16[768,768]{1,0:T(8,128)(2,1)} %self_hbm.1, ...), custom_call_target="tpu_custom_call" | custom-call | flops 7197425664 | bytes 9437184 | tf_op jit(solution)/shard_map/relational_layer/pallas_call | solution.py:270
  38.7 1.6 %copy.10 = bf16[128,768]{1,0:T(8,128)(2,1)} copy(bf16[128,768]{1,0:T(8,128)(2,1)} %relational_layer.1) | data formatting | bytes 393216
